TPU v7x, 128 devices: a whole 4x4x4 slice. The times are simulated.
128 devices in a mesh: wide: 8 (over x, core), sub: 16 (over z, y).
Axes of the slice: x: 4, y: 4, z: 4, core: 2. Of those that a mesh axis runs over, the one named last changes fastest.
Arguments:
- weights: bfloat16 [16384, 128, 128], P(('wide', 'sub')), may hold values from -6 to 6
- tables: bfloat16 [8, 16, 128, 128], replicated, may hold values from -0.375 to 0.375
- pattern_first: int32 [4, 16384, 2], P(None, ('wide', 'sub')), may hold values from 0 to 15
- pattern_second: int32 [4, 16384, 2], P(None, ('wide', 'sub')), may hold values from 0 to 15
Outputs:
- result: bfloat16 [16384, 128, 128], P(('wide', 'sub'))
All inputs are finite; a program needn't handle non-finite values.
Results may differ from a plain program's by a relative error of at most 0.0086.
Values may be sent and summed in bfloat16 or wider, within the bound.
No kernel may reach another device: no remote copies, remote signals or barrier semaphores. Data moves between devices by JAX's collectives and lax.ppermute only.
A program may use at most 128 MiB of HBM per device.

v0:
```python
import jax
import jax.numpy as jnp
from jax import lax
from jax.sharding import PartitionSpec as P


def swapped(value, axis, apart):
    return lax.ppermute(value, axis, [(i, i ^ 1 << apart) for i in range(lax.axis_size(axis))])


def combine_level(local_rows, far_rows, level_table, picks):
    block_own = jnp.take(level_table, picks[:, 0], axis=0)
    block_far = jnp.take(level_table, picks[:, 1], axis=0)
    summed = jnp.einsum("bcr,brs->bcs", local_rows, block_own, preferred_element_type=jnp.float32)
    summed = summed + jnp.einsum(
        "bcr,brs->bcs", far_rows, block_far, preferred_element_type=jnp.float32
    )
    return summed.astype(jnp.bfloat16)


def far_partner(rows, bit):
    return swapped(rows, ("wide", "sub"), bit)


def local(weights, tables, pattern_first, pattern_second):
    current = weights
    levels = pattern_first.shape[0]
    box_local = current.shape[0]
    for level_idx in range(levels):
        partner = far_partner(current, level_idx)
        current = combine_level(current, partner, tables[level_idx], pattern_first[level_idx])
    current = lax.all_to_all(current, ("wide", "sub"), split_axis=0, concat_axis=0, tiled=True)
    for level_idx in range(levels):
        flip = box_local // 2 ** (level_idx + 1)
        shaped = current.reshape((box_local // (2 * flip), 2, flip) + current.shape[1:])
        partner = jnp.flip(shaped, 1).reshape(current.shape)
        current = combine_level(
            current, partner, tables[levels + level_idx], pattern_second[level_idx]
        )
    return current


def solution(mesh):
    in_specs = (
        P(("wide", "sub"), None, None),
        P(),
        P(None, ("wide", "sub"), None),
        P(None, ("wide", "sub"), None),
    )
    out_specs = P(("wide", "sub"), None, None)
    return jax.shard_map(local, mesh=mesh, in_specs=in_specs, out_specs=out_specs, check_vma=False)
```

profile of v0, /device:TPU:1, one launch (start us, length us, event | category | flops | bytes accessed | tf_op | source)
XLA Modules:
  0.0 526.1 jit_solution(14685071558927230312)
XLA Ops:
  0.0 2.1 collective-permute-start
  2.1 0.7 slice_bitcast_fusion.12
  2.9 3.7 slice_bitcast_fusion
  6.5 4.1 gather_fusion
  10.7 4.1 gather_fusion.1
  14.8 9.9 %fusion.30 = f32[128,128,128]{2,1,0:T(8,128)} fusion(bf16[128,128,128]{2,1,0:T(8,128)(2,1)} %param.6, bf16[128,128,128]{2,1,0:T(8,128)(2,1)} %gather_fusion, pred[128]{0:T(512)(128)(4,1)S(1)} %get-tuple-element.68), kind=kOutput, calls=%fused_computation.54 | convolution fusion | flops 538968064 | bytes 16777344 | tf_op jit(solution)/shard_map/bcr,brs->bcs/dot_general | solution.py:14
  24.7 67.6 %collective-permute-done = bf16[128,128,128]{2,1,0:T(8,128)(2,1)} collective-permute-done((bf16[128,128,128]{2,1,0:T(8,128)(2,1)}, bf16[128,128,128]{2,1,0:T(8,128)(2,1)}, u32[]{:S(2)}, u32[]{:S(2)}) %collective-permute-start) | collective-permute-done | bytes 4194336 | tf_op jit(solution)/shard_map/ppermute | solution.py:8
  92.3 11.1 %add_convert_fusion.7 = bf16[128,128,128]{2,1,0:T(8,128)(2,1)} fusion(f32[128,128,128]{2,1,0:T(8,128)} %fusion.30, bf16[128,128,128]{2,1,0:T(8,128)(2,1)} %collective-permute-done, bf16[128,128,128]{2,1,0:T(8,128)(2,1)} %gather_fusion.1, pred[128]{0:T(512)(128)(4,1)S(1)} %get-tuple-element.34), kind=kOutput, calls=%fused_computation.23 | convolution fusion | flops 543162368 | bytes 20971648 | tf_op jit(solution)/shard_map/bcr,brs->bcs/dot_general | solution.py:15
  103.4 3.6 collective-permute-start.1
  107.0 4.1 gather_fusion.2
  111.1 4.1 gather_fusion.3
  115.2 8.5 %fusion.26 = f32[128,128,128]{2,1,0:T(8,128)} fusion(bf16[128,128,128]{2,1,0:T(8,128)(2,1)} %add_convert_fusion.7, bf16[128,128,128]{2,1,0:T(8,128)(2,1)} %gather_fusion.2, pred[128]{0:T(512)(128)(4,1)S(1)} %get-tuple-element.66), kind=kOutput, calls=%fused_computation.50 | convolution fusion | flops 538968064 | bytes 16777344 | tf_op jit(solution)/shard_map/bcr,brs->bcs/dot_general | solution.py:14
  123.7 72.8 %collective-permute-done.1 = bf16[128,128,128]{1,2,0:T(8,128)(2,1)} collective-permute-done((bf16[128,128,128]{1,2,0:T(8,128)(2,1)}, bf16[128,128,128]{1,2,0:T(8,128)(2,1)}, u32[]{:S(2)}, u32[]{:S(2)}) %collective-permute-start.1) | collective-permute-done | bytes 4194336 | tf_op jit(solution)/shard_map/ppermute | solution.py:8
  196.5 8.7 %add_convert_fusion.6 = bf16[128,128,128]{2,1,0:T(8,128)(2,1)} fusion(f32[128,128,128]{2,1,0:T(8,128)} %fusion.26, bf16[128,128,128]{1,2,0:T(8,128)(2,1)} %collective-permute-done.1, bf16[128,128,128]{2,1,0:T(8,128)(2,1)S(1)} %copy-done.4, pred[128]{0:T(512)(128)(4,1)S(1)} %get-tuple-element.30), kind=kOutput, calls=%fused_computation.22 | convolution fusion | flops 543162368 | bytes 20971648 | tf_op jit(solution)/shard_map/bcr,brs->bcs/dot_general | solution.py:15
  205.2 1.6 collective-permute-start.2
  206.8 3.1 gather_fusion.4
  209.9 3.1 gather_fusion.5
  212.9 4.9 fusion.22
  217.9 77.5 %collective-permute-done.2 = bf16[128,128,128]{2,1,0:T(8,128)(2,1)} collective-permute-done((bf16[128,128,128]{2,1,0:T(8,128)(2,1)}, bf16[128,128,128]{2,1,0:T(8,128)(2,1)}, u32[]{:S(2)}, u32[]{:S(2)}) %collective-permute-start.2) | collective-permute-done | bytes 4194336 | tf_op jit(solution)/shard_map/ppermute | solution.py:8
  295.4 6.0 %add_convert_fusion.5 = bf16[128,128,128]{2,1,0:T(8,128)(2,1)} fusion(f32[128,128,128]{2,1,0:T(8,128)S(1)} %fusion.22, bf16[128,128,128]{2,1,0:T(8,128)(2,1)} %collective-permute-done.2, bf16[128,128,128]{2,1,0:T(8,128)(2,1)S(1)} %copy-done.5, pred[128]{0:T(512)(128)(4,1)S(1)} %get-tuple-element.26), kind=kOutput, calls=%fused_computation.21 | convolution fusion | flops 543162368 | bytes 20971648 | tf_op jit(solution)/shard_map/bcr,brs->bcs/dot_general | solution.py:15
  301.4 3.2 collective-permute-start.3
  304.6 3.1 gather_fusion.6
  307.7 3.1 gather_fusion.7
  310.8 4.9 fusion.18
  315.7 76.7 %collective-permute-done.3 = bf16[128,128,128]{2,1,0:T(8,128)(2,1)} collective-permute-done((bf16[128,128,128]{2,1,0:T(8,128)(2,1)}, bf16[128,128,128]{2,1,0:T(8,128)(2,1)}, u32[]{:S(2)}, u32[]{:S(2)}) %collective-permute-start.3) | collective-permute-done | bytes 4194336 | tf_op jit(solution)/shard_map/ppermute | solution.py:8
  392.4 6.0 %add_convert_fusion.4 = bf16[128,128,128]{2,1,0:T(8,128)(2,1)} fusion(f32[128,128,128]{2,1,0:T(8,128)S(1)} %fusion.18, bf16[128,128,128]{2,1,0:T(8,128)(2,1)} %collective-permute-done.3, bf16[128,128,128]{2,1,0:T(8,128)(2,1)S(1)} %copy-done.6, pred[128]{0:T(512)(128)(4,1)S(1)} %get-tuple-element.22), kind=kOutput, calls=%fused_computation.20 | convolution fusion | flops 543162368 | bytes 20971648 | tf_op jit(solution)/shard_map/bcr,brs->bcs/dot_general | solution.py:15
  398.4 14.0 %all-to-all-start = ((bf16[128,128,128]{2,1,0:T(8,128)(2,1)}), bf16[128,128,128]{2,1,0:T(8,128)(2,1)}, u32[]{:S(2)}, u32[]{:S(2)}) async-start(bf16[128,128,128]{2,1,0:T(8,128)(2,1)} %add_convert_fusion.4), calls=%async_computation | async-start | bytes 8388608 | tf_op jit(solution)/shard_map/all_to_all | solution.py:32
  412.5 3.0 gather_fusion.9
  415.5 3.2 gather_fusion.8
  418.7 3.1 gather_fusion.11
  421.7 3.1 gather_fusion.10
  424.8 3.0 gather_fusion.13
  427.9 3.1 gather_fusion.12
  430.9 3.1 gather_fusion.15
  434.0 3.0 gather_fusion.14
  437.0 25.9 %all-to-all-done = bf16[128,128,128]{2,1,0:T(8,128)(2,1)} async-done(((bf16[128,128,128]{2,1,0:T(8,128)(2,1)}), bf16[128,128,128]{2,1,0:T(8,128)(2,1)}, u32[]{:S(2)}, u32[]{:S(2)}) %all-to-all-start) | async-done | bytes 4194336 | tf_op jit(solution)/shard_map/all_to_all | solution.py:32
  462.9 4.8 rev.16
  467.7 4.9 fusion.12
  472.6 6.0 %add_convert_fusion.3 = bf16[128,128,128]{2,1,0:T(8,128)(2,1)} fusion(f32[128,128,128]{2,1,0:T(8,128)S(1)} %fusion.12, bf16[128,128,128]{2,1,0:T(8,128)(2,1)} %all-to-all-done, bf16[128,128,128]{2,1,0:T(8,128)(2,1)S(1)} %copy-done.3, pred[128]{0:T(512)(128)(4,1)S(1)} %get-tuple-element.76), kind=kOutput, calls=%fused_computation.19 | convolution fusion | flops 543162368 | bytes 20971648 | tf_op jit(solution)/shard_map/bcr,brs->bcs/dot_general | solution.py:14
  478.6 4.7 rev.17
  483.3 4.9 fusion.8
  488.3 6.0 %add_convert_fusion.2 = bf16[128,128,128]{2,1,0:T(8,128)(2,1)} fusion(f32[128,128,128]{2,1,0:T(8,128)S(1)} %fusion.8, bf16[128,128,128]{2,1,0:T(8,128)(2,1)S(1)} %copy-done, bf16[128,128,128]{2,1,0:T(8,128)(2,1)} %gather_fusion.10, pred[128]{0:T(512)(128)(4,1)S(1)} %get-tuple-element.14), kind=kOutput, calls=%fused_computation.18 | convolution fusion | flops 543162368 | bytes 20971648 | tf_op jit(solution)/shard_map/bcr,brs->bcs/dot_general | solution.py:14
  494.3 4.7 rev.18
  499.0 5.2 fusion.4
  504.2 6.0 %add_convert_fusion.1 = bf16[128,128,128]{2,1,0:T(8,128)(2,1)} fusion(f32[128,128,128]{2,1,0:T(8,128)S(1)} %fusion.4, bf16[128,128,128]{2,1,0:T(8,128)(2,1)S(1)} %copy-done.2, bf16[128,128,128]{2,1,0:T(8,128)(2,1)} %gather_fusion.12, pred[128]{0:T(512)(128)(4,1)S(1)} %get-tuple-element.72), kind=kOutput, calls=%fused_computation.17 | convolution fusion | flops 543162368 | bytes 20971648 | tf_op jit(solution)/shard_map/bcr,brs->bcs/dot_general | solution.py:14
  510.2 4.7 rev.19
  514.9 4.9 fusion
  519.9 6.0 %add_convert_fusion = bf16[128,128,128]{2,1,0:T(8,128)(2,1)} fusion(f32[128,128,128]{2,1,0:T(8,128)S(1)} %fusion, bf16[128,128,128]{2,1,0:T(8,128)(2,1)S(1)} %copy-done.1, bf16[128,128,128]{2,1,0:T(8,128)(2,1)} %gather_fusion.14, pred[128]{0:T(512)(128)(4,1)S(1)} %get-tuple-element.6), kind=kOutput, calls=%fused_computation.16 | convolution fusion | flops 543162368 | bytes 20971648 | tf_op jit(solution)/shard_map/bcr,brs->bcs/dot_general | solution.py:14
  (39 shorter events, 0.2 us)
Async XLA Ops:
  0.0 92.3 %collective-permute-start = (bf16[128,128,128]{2,1,0:T(8,128)(2,1)}, bf16[128,128,128]{2,1,0:T(8,128)(2,1)}, u32[]{:S(2)}, u32[]{:S(2)}) collective-permute-start(bf16[128,128,128]{2,1,0:T(8,128)(2,1)} %param.6), channel_id=1, source_target_pairs={{0,1},{1,0},{2,3},{3,2},{4,5},{5,4},{6,7},{7,6},{8,9},{9,8},{10,11... | collective-permute-start | bytes 12582920 | tf_op jit(solution)/shard_map/ppermute | solution.py:8
  103.4 93.1 %collective-permute-start.1 = (bf16[128,128,128]{1,2,0:T(8,128)(2,1)}, bf16[128,128,128]{1,2,0:T(8,128)(2,1)}, u32[]{:S(2)}, u32[]{:S(2)}) collective-permute-start(bf16[128,128,128]{1,2,0:T(8,128)(2,1)} %bitcast.112), channel_id=1, source_target_pairs={{0,2},{1,3},{2,0},{3,1},{4,6},{5,7},{6,4},{7,5},{8,10},{9,11},{10,... | collective-permute-start | bytes 12582920 | tf_op jit(solution)/shard_map/ppermute | solution.py:8
  115.1 81.3 %copy-start.4 = (bf16[128,128,128]{2,1,0:T(8,128)(2,1)S(1)}, bf16[128,128,128]{2,1,0:T(8,128)(2,1)}, u32[]{:S(2)}) copy-start(bf16[128,128,128]{2,1,0:T(8,128)(2,1)} %gather_fusion.3) | copy-start | bytes 12582916
  205.2 90.2 %collective-permute-start.2 = (bf16[128,128,128]{2,1,0:T(8,128)(2,1)}, bf16[128,128,128]{2,1,0:T(8,128)(2,1)}, u32[]{:S(2)}, u32[]{:S(2)}) collective-permute-start(bf16[128,128,128]{2,1,0:T(8,128)(2,1)} %add_convert_fusion.6), channel_id=1, source_target_pairs={{0,4},{1,5},{2,6},{3,7},{4,0},{5,1},{6,2},{7,3},{8,12},{9,13},{10,... | collective-permute-start | bytes 12582920 | tf_op jit(solution)/shard_map/ppermute | solution.py:8
  212.9 82.5 %copy-start.5 = (bf16[128,128,128]{2,1,0:T(8,128)(2,1)S(1)}, bf16[128,128,128]{2,1,0:T(8,128)(2,1)}, u32[]{:S(2)}) copy-start(bf16[128,128,128]{2,1,0:T(8,128)(2,1)} %gather_fusion.5) | copy-start | bytes 12582916
  301.4 91.0 %collective-permute-start.3 = (bf16[128,128,128]{2,1,0:T(8,128)(2,1)}, bf16[128,128,128]{2,1,0:T(8,128)(2,1)}, u32[]{:S(2)}, u32[]{:S(2)}) collective-permute-start(bf16[128,128,128]{2,1,0:T(8,128)(2,1)} %add_convert_fusion.5), channel_id=1, source_target_pairs={{0,8},{1,9},{2,10},{3,11},{4,12},{5,13},{6,14},{7,15},{8,0},{9,1},... | collective-permute-start | bytes 12582920 | tf_op jit(solution)/shard_map/ppermute | solution.py:8
  310.8 81.6 %copy-start.6 = (bf16[128,128,128]{2,1,0:T(8,128)(2,1)S(1)}, bf16[128,128,128]{2,1,0:T(8,128)(2,1)}, u32[]{:S(2)}) copy-start(bf16[128,128,128]{2,1,0:T(8,128)(2,1)} %gather_fusion.7) | copy-start | bytes 12582916
  398.4 14.0 %copy-start.7 = (s32[4,128,2]{1,2,0:T(2,128)S(1)}, s32[4,128,2]{1,2,0:T(2,128)}, u32[]{:S(2)}) copy-start(s32[4,128,2]{1,2,0:T(2,128)} %param.9) | copy-start | bytes 12292
  398.4 64.5 %all-to-all-start = ((bf16[128,128,128]{2,1,0:T(8,128)(2,1)}), bf16[128,128,128]{2,1,0:T(8,128)(2,1)}, u32[]{:S(2)}, u32[]{:S(2)}) async-start(bf16[128,128,128]{2,1,0:T(8,128)(2,1)} %add_convert_fusion.4), calls=%async_computation | async-start | bytes 8388608 | tf_op jit(solution)/shard_map/all_to_all | solution.py:32
  467.7 4.9 copy-start.3
  483.3 4.9 copy-start
  499.0 5.2 copy-start.2
  514.9 4.9 copy-start.1
where the time goes:
time: 533 us; the launch traced here: 526 us
  waiting for transfers between devices  321 us (60%)
  matrix products  104 us (20%)
  local copies, waits for them, and re-layouts  76.5 us (14%)
  starting transfers between devices  24.6 us (5%)
    ppermute x4, waiting for transfers between devices, swapped(): lax.ppermute(value, axis, [(i, i ^ 1 << apart) for i in range(lax.axis_si...  295 us
    dot_general x8, matrix products, combine_level(): jnp.einsum('bcr,brs->bcs', local_rows, block_own, preferred_element_type=...  52.3 us
    dot_general x8, matrix products, combine_level(): jnp.einsum('bcr,brs->bcs', far_rows, block_far, preferred_element_type=jn...  51.6 us
    gather x8, local copies, waits for them, and re-layouts, combine_level(): block_own = jnp.take(level_table, picks[:, 0], axis=0)  26.7 us
    gather x8, local copies, waits for them, and re-layouts, combine_level(): block_far = jnp.take(level_table, picks[:, 1], axis=0)  26.4 us
    all_to_all x1, waiting for transfers between devices, local(): lax.all_to_all(current, ('wide', 'sub'), split_axis=0, concat_axis=0, til...  25.9 us
    rev x4, local copies, waits for them, and re-layouts, local(): partner = jnp.flip(shaped, 1).reshape(current.shape)  18.9 us
    all_to_all x1, starting transfers between devices, local(): lax.all_to_all(current, ('wide', 'sub'), split_axis=0, concat_axis=0, til...  14 us
  transfers between devices with their start and end apart: 5, of which 5 were waited for; matrix products, arithmetic and copies ran while one was open for 16% of the time, Pallas kernels for 0%

commit v1 on v0

v1 whole, which is shorter than its diff:
```python
import jax
import jax.numpy as jnp
from jax import lax
from jax.experimental import pallas as pl
from jax.experimental.pallas import tpu as pltpu
from jax.sharding import PartitionSpec as P

AXES = ("wide", "sub")


def butterfly(first, second, tables, data, out, *, flips):
    boxes = data.shape[0]
    levels = len(flips) // 2

    def pick(level, term, box):
        if level < levels:
            return first[box, 2 * level + term]
        return second[2 * (level - levels) + term, box]

    for level, flip in enumerate(flips):
        source = data if level == 0 else out

        def pair(index, _, level=level, flip=flip, source=source):
            low = (index // flip) * (2 * flip) + index % flip
            high = low + flip
            rows = jnp.concatenate([source[low], source[high]], axis=1)
            own = [tables[level, pick(level, 0, low)], tables[level, pick(level, 0, high)]]
            far = [tables[level, pick(level, 1, low)], tables[level, pick(level, 1, high)]]
            blocks = jnp.concatenate(
                [jnp.concatenate([own[0], far[1]], axis=1), jnp.concatenate([far[0], own[1]], axis=1)], axis=0
            )
            summed = jnp.dot(rows, blocks, preferred_element_type=jnp.float32).astype(jnp.bfloat16)
            cols = summed.shape[1] // 2
            out[low] = summed[:, :cols]
            out[high] = summed[:, cols:]
            return 0

        lax.fori_loop(0, boxes // 2, pair, 0, unroll=4)


def local(weights, tables, pattern_first, pattern_second):
    levels = pattern_first.shape[0]
    boxes = weights.shape[0]
    first = pattern_first.transpose(1, 0, 2).reshape(boxes, 2 * levels)
    first = lax.all_to_all(first, AXES, split_axis=0, concat_axis=0, tiled=True)
    current = lax.all_to_all(weights, AXES, split_axis=0, concat_axis=0, tiled=True)
    second = pattern_second.transpose(0, 2, 1).reshape(2 * levels, boxes)
    flips = [2**level for level in range(levels)] + [boxes // 2 ** (level + 1) for level in range(levels)]
    smem = pl.BlockSpec(memory_space=pltpu.SMEM)
    vmem = pl.BlockSpec(memory_space=pltpu.VMEM)
    return pl.pallas_call(
        lambda *refs: butterfly(*refs, flips=flips),
        out_shape=jax.ShapeDtypeStruct(current.shape, current.dtype),
        in_specs=[smem, smem, vmem, vmem],
        out_specs=vmem,
        compiler_params=pltpu.CompilerParams(vmem_limit_bytes=40 * 2**20),
        cost_estimate=pl.CostEstimate(
            flops=2 * levels * boxes * 2 * 2 * 128**3, bytes_accessed=12 * 2**20, transcendentals=0
        ),
    )(first, second, tables, current)


def solution(mesh):
    in_specs = (
        P(AXES, None, None),
        P(),
        P(None, AXES, None),
        P(None, AXES, None),
    )
    out_specs = P(AXES, None, None)
    return jax.shard_map(local, mesh=mesh, in_specs=in_specs, out_specs=out_specs, check_vma=False)
```

time: 533 us -> 158 us (0.30); the launches traced: 526 us -> 157 us
  waiting for transfers between devices: 321 us -> 0 us
  matrix products: 104 us -> 0 us
  Pallas kernels: 0 us -> 79.1 us
  blocking collectives: 0 us -> 77.2 us
  local copies, waits for them, and re-layouts: 76.5 us -> 0.79 us
  starting transfers between devices: 24.6 us -> 0 us
    ppermute x4 -> x0, waiting for transfers between devices: 295 us -> none  [swapped(): lax.ppermute(value, axis, [(i, i ^ 1 << apart) for i in range(lax.axis_si...]
    dot_general x16 -> x0, matrix products: 104 us -> none  [the longest x8 52.3 us: combine_level(): jnp.einsum('bcr,brs->bcs', local_rows, block_own, preferred_element_type=...]
    pallas_call x0 -> x1, Pallas kernels: none -> 79.1 us  [local(): pl.pallas_call(lambda *refs: butterfly(*refs, flips=flips), out_shape=jax...]
    all_to_all x0 -> x2, blocking collectives: none -> 77.2 us  [the longest x1 56.1 us: local(): lax.all_to_all(weights, AXES, split_axis=0, concat_axis=0, tiled=True)]
    gather x16 -> x0, local copies, waits for them, and re-layouts: 53.1 us -> none  [the longest x8 26.7 us: combine_level(): block_own = jnp.take(level_table, picks[:, 0], axis=0)]
    all_to_all x1 -> x0, waiting for transfers between devices: 25.9 us -> none  [local(): lax.all_to_all(current, ('wide', 'sub'), split_axis=0, concat_axis=0, til...]
    rev x4 -> x0, local copies, waits for them, and re-layouts: 18.9 us -> none  [local(): partner = jnp.flip(shaped, 1).reshape(current.shape)]
    all_to_all x1 -> x0, starting transfers between devices: 14 us -> none  [local(): lax.all_to_all(current, ('wide', 'sub'), split_axis=0, concat_axis=0, til...]
  transfers between devices with their start and end apart: 5 -> 0, of which waited for: 5 -> 0; matrix products, arithmetic and copies ran while one was open for 16% -> 0% of each run, Pallas kernels for 0% -> 0%
where the time goes in v1:
time: 158 us; the launch traced here: 157 us
  Pallas kernels  79.1 us (50%)
  blocking collectives  77.2 us (49%)
    pallas_call x1, Pallas kernels, local(): pl.pallas_call(lambda *refs: butterfly(*refs, flips=flips), out_shape=jax...  79.1 us
    all_to_all x1, blocking collectives, local(): lax.all_to_all(weights, AXES, split_axis=0, concat_axis=0, tiled=True)  56.1 us
    all_to_all x1, blocking collectives, local(): first = lax.all_to_all(first, AXES, split_axis=0, concat_axis=0, tiled=True)  21.1 us

profile of v1, /device:TPU:1, one launch (start us, length us, event | category | flops | bytes accessed | tf_op | source)
XLA Modules:
  0.0 157.2 jit_solution(12633475505454198637)
XLA Ops:
  0.0 0.8 copy.7
  0.8 21.1 %all_to_all.16 = s32[128,1,8]{2,1,0:T(1,128)S(1)} all-to-all(s32[128,1,8]{2,1,0:T(1,128)S(1)} %copy.7), channel_id=1, replica_groups=mesh['wide'=8,'sub'=16] {'wide','sub'}, dimensions={0} | all-to-all | bytes 8192 | tf_op jit(solution)/shard_map/all_to_all | solution.py:45
  21.9 0.0 copy-start
  21.9 0.0 copy-start.1
  21.9 56.1 %all_to_all.17.refs_3_ = bf16[128,128,128]{2,1,0:T(8,128)(2,1)S(1)} all-to-all(bf16[128,128,128]{2,1,0:T(8,128)(2,1)} %param.4), channel_id=1, replica_groups=mesh['wide'=8,'sub'=16] {'wide','sub'}, dimensions={0} | all-to-all | bytes 8388608 | tf_op jit(solution)/shard_map/all_to_all | solution.py:46
  78.0 0.0 copy-done
  78.0 0.0 copy-done.1
  78.0 79.1 %shard_map.46 = bf16[128,128,128]{2,1,0:T(8,128)(2,1)} custom-call(s32[128,8]{1,0:T(8,128)S(1)} %bitcast.7, s32[8,128]{1,0:T(8,128)S(1)} %bitcast.8, bf16[8,16,128,128]{3,2,1,0:T(8,128)(2,1)S(1)} %copy-done, bf16[128,128,128]{2,1,0:T(8,128)(2,1)S(1)} %all_to_all.17.refs_3_), custom_call_target="tpu_custom_call" | custom-call | flops 8589934592 | bytes 12582912 | tf_op jit(solution)/shard_map/pallas_call | solution.py:51
Async XLA Ops:
  21.9 56.2 %copy-start = (bf16[8,16,128,128]{3,2,1,0:T(8,128)(2,1)S(1)}, bf16[8,16,128,128]{3,2,1,0:T(8,128)(2,1)}, u32[]{:S(2)}) copy-start(bf16[8,16,128,128]{3,2,1,0:T(8,128)(2,1)} %refs_2_.1) | copy-start | bytes 12582916
  21.9 56.2 %copy-start.1 = (s32[4,128,2]{1,2,0:T(2,128)S(1)}, s32[4,128,2]{1,2,0:T(2,128)}, u32[]{:S(2)}) copy-start(s32[4,128,2]{1,2,0:T(2,128)} %param.7) | copy-start | bytes 12292

commit v2 on v1

v2 whole, which is shorter than its diff:
```python
import jax
import jax.numpy as jnp
from jax import lax
from jax.experimental import pallas as pl
from jax.experimental.pallas import tpu as pltpu
from jax.sharding import PartitionSpec as P

AXES = ("wide", "sub")


def butterfly(first, second, tables, data, out, blocks, here, there, table_done, data_done, out_done, *, levels):
    boxes, cols = data.shape[0], data.shape[2]
    span = 2**levels
    apart = boxes // span
    half = boxes // 2

    def table_copy(level):
        return pltpu.make_async_copy(tables.at[level], blocks.at[level], table_done.at[level])

    def data_copy(part):
        where = pl.ds(part * half, half)
        return pltpu.make_async_copy(data.at[where], here.at[where], data_done.at[part])

    def out_copy(part, row):
        where = pl.ds(row * apart + part * (apart // 2), apart // 2)
        return pltpu.make_async_copy(here.at[where], out.at[where], out_done.at[part])

    table_copy(0).start()
    for part in range(2):
        data_copy(part).start()
    for level in range(1, 2 * levels):
        table_copy(level).start()

    def combine(level, pairs, source, target, pick):
        done = []
        for low, high in pairs:
            rows = jnp.concatenate([source[low], source[high]], axis=1)
            own = [blocks[level, pick(0, box)] for box in (low, high)]
            far = [blocks[level, pick(1, box)] for box in (low, high)]
            square = jnp.concatenate(
                [jnp.concatenate([own[0], far[1]], axis=1), jnp.concatenate([far[0], own[1]], axis=1)], axis=0
            )
            done.append(jnp.dot(rows, square, preferred_element_type=jnp.float32).astype(jnp.bfloat16))
        for (low, high), summed in zip(pairs, done):
            target[low] = summed[:, :cols]
            target[high] = summed[:, cols:]

    def split(index, flip):
        return (index // flip) * (2 * flip) + index % flip

    def before(part, _):
        data_copy(part).wait()
        for level in range(levels):
            @pl.when(part == 0)
            def _():
                table_copy(level).wait()

            source, target = (there, here) if level % 2 else (here, there)
            flip = 2**level
            lows = [part * half + split(pair, flip) for pair in range(half // 2)]
            combine(
                level,
                [(low, low + flip) for low in lows],
                source,
                target,
                lambda term, box: first[box, 2 * level + term],
            )
        return 0

    def after(part, _):
        for step in range(levels):
            level = levels + step

            @pl.when(part == 0)
            def _():
                table_copy(level).wait()

            source, target = (there, here) if level % 2 else (here, there)
            flip = span // 2 ** (step + 1)
            lows = [
                split(pair // (apart // 2), flip) * apart + part * (apart // 2) + pair % (apart // 2)
                for pair in range(half // 2)
            ]
            combine(
                level,
                [(low, low + flip * apart) for low in lows],
                source,
                target,
                lambda term, box: second[2 * step + term, box],
            )
        for row in range(span):
            out_copy(part, row).start()
        return 0

    lax.fori_loop(0, 2, before, 0)
    lax.fori_loop(0, 2, after, 0)
    for part in range(2):
        for row in range(span):
            out_copy(part, row).wait()


def local(weights, tables, pattern_first, pattern_second):
    levels, boxes = pattern_first.shape[0], weights.shape[0]
    current = lax.all_to_all(weights, AXES, split_axis=0, concat_axis=0, tiled=True)
    first = lax.all_gather(pattern_first.transpose(0, 2, 1).reshape(2 * levels, boxes), AXES)
    first = lax.dynamic_slice_in_dim(first, lax.axis_index(AXES), 1, axis=2)[:, :, 0]
    second = pattern_second.transpose(0, 2, 1).reshape(2 * levels, boxes)
    smem = pl.BlockSpec(memory_space=pltpu.SMEM)
    hbm = pl.BlockSpec(memory_space=pltpu.HBM)
    return pl.pallas_call(
        lambda *refs: butterfly(*refs, levels=levels),
        out_shape=jax.ShapeDtypeStruct(current.shape, current.dtype),
        in_specs=[smem, smem, hbm, hbm],
        out_specs=hbm,
        scratch_shapes=[
            pltpu.VMEM(tables.shape, tables.dtype),
            pltpu.VMEM(current.shape, current.dtype),
            pltpu.VMEM(current.shape, current.dtype),
            pltpu.SemaphoreType.DMA((2 * levels,)),
            pltpu.SemaphoreType.DMA((2,)),
            pltpu.SemaphoreType.DMA((2,)),
        ],
        compiler_params=pltpu.CompilerParams(vmem_limit_bytes=40 * 2**20),
        cost_estimate=pl.CostEstimate(
            flops=2 * levels * boxes * 2 * 2 * 128**3, bytes_accessed=12 * 2**20, transcendentals=0
        ),
    )(first, second, tables, current)


def solution(mesh):
    in_specs = (
        P(AXES, None, None),
        P(),
        P(None, AXES, None),
        P(None, AXES, None),
    )
    out_specs = P(AXES, None, None)
    return jax.shard_map(local, mesh=mesh, in_specs=in_specs, out_specs=out_specs, check_vma=False)
```

time: 158 us -> 126 us (0.80)
  Pallas kernels: 79.1 us -> 18.9 us
  blocking collectives: 77.2 us -> 90.9 us
  starting transfers between devices: 0 us -> 12 us
  local copies, waits for them, and re-layouts: 0.79 us -> 3.21 us
    all_gather x0 -> x1, blocking collectives: none -> 90.9 us  [local(): lax.all_gather(pattern_first.transpose(0, 2, 1).reshape(2 * levels, boxes...]
    all_to_all x2 -> x0, blocking collectives: 77.2 us -> none  [the longest x1 56.1 us: local(): lax.all_to_all(weights, AXES, split_axis=0, concat_axis=0, tiled=True)]
    pallas_call x1, Pallas kernels: 79.1 us -> 18.9 us  [local(): pl.pallas_call(lambda *refs: butterfly(*refs, levels=levels), out_shape=j...]
    all_to_all x0 -> x1, starting transfers between devices: none -> 12 us  [local(): lax.all_to_all(weights, AXES, split_axis=0, concat_axis=0, tiled=True)]
    unnamed x4 -> x6, local copies, waits for them, and re-layouts: 0.01 us -> 2.2 us
  transfers between devices with their start and end apart: 0 -> 1, of which waited for: 0 -> 0; matrix products, arithmetic and copies ran while one was open for 0% -> 1% of each run, Pallas kernels for 0% -> 0%
where the time goes in v2:
time: 126 us; the launch traced here: 125 us
  blocking collectives  90.9 us (72%)
  Pallas kernels  18.9 us (15%)
  starting transfers between devices  12 us (10%)
  local copies, waits for them, and re-layouts  3.21 us (3%)
    all_gather x1, blocking collectives, local(): lax.all_gather(pattern_first.transpose(0, 2, 1).reshape(2 * levels, boxes...  90.9 us
    pallas_call x1, Pallas kernels, local(): pl.pallas_call(lambda *refs: butterfly(*refs, levels=levels), out_shape=j...  18.9 us
    all_to_all x1, starting transfers between devices, local(): lax.all_to_all(weights, AXES, split_axis=0, concat_axis=0, tiled=True)  12 us
  transfers between devices with their start and end apart: 1, of which 0 were waited for; matrix products, arithmetic and copies ran while one was open for 1% of the time, Pallas kernels for 0%

profile of v2, /device:TPU:1, one launch (start us, length us, event | category | flops | bytes accessed | tf_op | source)
XLA Modules:
  0.0 125.0 jit_solution(8804821759130566503)
XLA Ops:
  0.0 0.0 copy-start.2
  0.0 0.0 copy-start.1
  0.0 12.0 %all-to-all-start = ((bf16[128,128,128]{2,1,0:T(8,128)(2,1)}), bf16[128,128,128]{2,1,0:T(8,128)(2,1)}, u32[]{:S(2)}, u32[]{:S(2)}) async-start(bf16[128,128,128]{2,1,0:T(8,128)(2,1)} %param.4), calls=%async_computation | async-start | bytes 8388608 | tf_op jit(solution)/shard_map/all_to_all | solution.py:104
  12.0 0.0 copy-done.2
  12.0 90.9 %all_gather.3 = s32[128,8,128]{2,1,0:T(8,128)S(1)} all-gather(s32[1,8,128]{2,1,0:T(8,128)S(1)} %bitcast.10), channel_id=1, replica_groups=mesh['wide'=8,'sub'=16] {'wide','sub'}, dimensions={0}, use_global_device_ids=true | all-gather | bytes 528384 | tf_op jit(solution)/shard_map/all_gather | solution.py:105
  102.9 0.2 constant_dynamic-slice_fusion
  103.1 0.8 copy.9
  103.9 0.0 all-to-all-done.refs_3_
  103.9 0.0 copy-done.1
  103.9 0.0 copy-start
  103.9 2.2 %copy-done = bf16[8,16,128,128]{3,2,1,0:T(8,128)(2,1)S(1)} copy-done((bf16[8,16,128,128]{3,2,1,0:T(8,128)(2,1)S(1)}, bf16[8,16,128,128]{3,2,1,0:T(8,128)(2,1)}, u32[]{:S(2)}) %copy-start) | copy-done | bytes 4194328
  106.1 18.9 %shard_map.46 = bf16[128,128,128]{2,1,0:T(8,128)(2,1)} custom-call(s32[128,8]{1,0:T(8,128)S(1)} %bitcast.8, s32[8,128]{1,0:T(8,128)S(1)} %bitcast.9, bf16[8,16,128,128]{3,2,1,0:T(8,128)(2,1)S(1)} %copy-done, bf16[128,128,128]{2,1,0:T(8,128)(2,1)} %all-to-all-done.refs_3_), custom_call_target="tpu_custom_call" | custom-call | flops 8589934592 | bytes 12582912 | tf_op jit(solution)/shard_map/pallas_call | solution.py:110
Async XLA Ops:
  0.0 12.0 %copy-start.2 = (s32[4,128,2]{1,2,0:T(2,128)S(1)}, s32[4,128,2]{1,2,0:T(2,128)}, u32[]{:S(2)}) copy-start(s32[4,128,2]{1,2,0:T(2,128)} %param.6) | copy-start | bytes 12292
  0.0 103.9 %copy-start.1 = (s32[4,128,2]{1,2,0:T(2,128)S(1)}, s32[4,128,2]{1,2,0:T(2,128)}, u32[]{:S(2)}) copy-start(s32[4,128,2]{1,2,0:T(2,128)} %param.7) | copy-start | bytes 12292
  0.0 103.9 %all-to-all-start = ((bf16[128,128,128]{2,1,0:T(8,128)(2,1)}), bf16[128,128,128]{2,1,0:T(8,128)(2,1)}, u32[]{:S(2)}, u32[]{:S(2)}) async-start(bf16[128,128,128]{2,1,0:T(8,128)(2,1)} %param.4), calls=%async_computation | async-start | bytes 8388608 | tf_op jit(solution)/shard_map/all_to_all | solution.py:104
  103.9 2.2 %copy-start = (bf16[8,16,128,128]{3,2,1,0:T(8,128)(2,1)S(1)}, bf16[8,16,128,128]{3,2,1,0:T(8,128)(2,1)}, u32[]{:S(2)}) copy-start(bf16[8,16,128,128]{3,2,1,0:T(8,128)(2,1)} %refs_2_.1) | copy-start | bytes 12582916

commit v3 on v2

v3 whole, which is shorter than its diff:
```python
import jax
import jax.numpy as jnp
from jax import lax
from jax.experimental import pallas as pl
from jax.experimental.pallas import tpu as pltpu
from jax.sharding import PartitionSpec as P

AXES = ("wide", "sub")
EXTRA = 8


def butterfly(first, second, tables, data, out, here, there, out_done, *, levels):
    boxes, count, cols = out.shape
    span = 2**levels
    apart = boxes // span
    half = boxes // 2

    def out_copy(part, row):
        where = pl.ds(row * apart + part * (apart // 2), apart // 2)
        return pltpu.make_async_copy(here.at[where], out.at[where], out_done.at[part])

    def combine(level, pairs, pick):
        source, target = (there, here) if level % 2 else (here if level else data, there)
        done = []
        for low, high in pairs:
            rows = jnp.concatenate([source[low, :count], source[high, :count]], axis=1)
            own = [tables[level, pick(0, box)] for box in (low, high)]
            far = [tables[level, pick(1, box)] for box in (low, high)]
            square = jnp.concatenate(
                [jnp.concatenate([own[0], far[1]], axis=1), jnp.concatenate([far[0], own[1]], axis=1)], axis=0
            )
            done.append(jnp.dot(rows, square, preferred_element_type=jnp.float32).astype(jnp.bfloat16))
        for (low, high), summed in zip(pairs, done):
            target[low] = summed[:, :cols]
            target[high] = summed[:, cols:]

    def split(index, flip):
        return (index // flip) * (2 * flip) + index % flip

    def before(part, _):
        for level in range(levels):
            flip = 2**level
            lows = [part * half + split(pair, flip) for pair in range(half // 2)]
            combine(level, [(low, low + flip) for low in lows], lambda term, box: first[box, 2 * level + term])
        return 0

    def after(part, _):
        for step in range(levels):
            flip = span // 2 ** (step + 1)
            lows = [
                split(pair // (apart // 2), flip) * apart + part * (apart // 2) + pair % (apart // 2)
                for pair in range(half // 2)
            ]
            combine(
                levels + step,
                [(low, low + flip * apart) for low in lows],
                lambda term, box: second[2 * step + term, box],
            )
        for row in range(span):
            out_copy(part, row).start()
        return 0

    lax.fori_loop(0, 2, before, 0)
    lax.fori_loop(0, 2, after, 0)
    for part in range(2):
        for row in range(span):
            out_copy(part, row).wait()


def local(weights, tables, pattern_first, pattern_second):
    levels = pattern_first.shape[0]
    boxes, count, cols = weights.shape
    picks = pattern_first.transpose(1, 0, 2).reshape(boxes, 1, 2 * levels).astype(jnp.bfloat16)
    picks = jnp.pad(picks, ((0, 0), (0, EXTRA - 1), (0, cols - 2 * levels)))
    current = jnp.concatenate([weights, picks], axis=1)
    current = lax.all_to_all(current, AXES, split_axis=0, concat_axis=0, tiled=True)
    first = current[:, count, : 2 * levels].astype(jnp.int32)
    second = pattern_second.transpose(0, 2, 1).reshape(2 * levels, boxes)
    smem = pl.BlockSpec(memory_space=pltpu.SMEM)
    vmem = pl.BlockSpec(memory_space=pltpu.VMEM)
    return pl.pallas_call(
        lambda *refs: butterfly(*refs, levels=levels),
        out_shape=jax.ShapeDtypeStruct(weights.shape, weights.dtype),
        in_specs=[smem, smem, vmem, vmem],
        out_specs=pl.BlockSpec(memory_space=pl.ANY),
        scratch_shapes=[
            pltpu.VMEM(weights.shape, weights.dtype),
            pltpu.VMEM(weights.shape, weights.dtype),
            pltpu.SemaphoreType.DMA((2,)),
        ],
        compiler_params=pltpu.CompilerParams(vmem_limit_bytes=40 * 2**20),
        cost_estimate=pl.CostEstimate(
            flops=2 * levels * boxes * 2 * 2 * 128**3, bytes_accessed=12 * 2**20, transcendentals=0
        ),
    )(first, second, tables, current)


def solution(mesh):
    in_specs = (
        P(AXES, None, None),
        P(),
        P(None, AXES, None),
        P(None, AXES, None),
    )
    out_specs = P(AXES, None, None)
    return jax.shard_map(local, mesh=mesh, in_specs=in_specs, out_specs=out_specs, check_vma=False)
```

time: 126 us -> 86.4 us (0.69)
  blocking collectives: 90.9 us -> 67.5 us
  starting transfers between devices: 12 us -> 0 us
  Pallas kernels: 18.9 us -> 15.4 us
  other arithmetic: 0 us -> 3.2 us
  local copies, waits for them, and re-layouts: 3.21 us -> 0.14 us
    all_gather x1 -> x0, blocking collectives: 90.9 us -> none  [local(): lax.all_gather(pattern_first.transpose(0, 2, 1).reshape(2 * levels, boxes...]
    all_to_all x0 -> x1, blocking collectives: none -> 67.5 us  [local(): lax.all_to_all(current, AXES, split_axis=0, concat_axis=0, tiled=True)]
    all_to_all x1 -> x0, starting transfers between devices: 12 us -> none  [local(): lax.all_to_all(weights, AXES, split_axis=0, concat_axis=0, tiled=True)]
    pallas_call x1, Pallas kernels: 18.9 us -> 15.4 us  [local(): pl.pallas_call(lambda *refs: butterfly(*refs, levels=levels), out_shape=j...]
    concatenate x0 -> x1, other arithmetic: none -> 2.46 us  [local(): current = jnp.concatenate([weights, picks], axis=1)]
    unnamed x6 -> x4, local copies, waits for them, and re-layouts: 2.2 us -> 0.01 us
  transfers between devices with their start and end apart: 1 -> 0, of which waited for: 0 -> 0; matrix products, arithmetic and copies ran while one was open for 1% -> 0% of each run, Pallas kernels for 0% -> 0%
where the time goes in v3:
time: 86.4 us; the launch traced here: 86.2 us
  blocking collectives  67.5 us (78%)
  Pallas kernels  15.4 us (18%)
  other arithmetic  3.2 us (4%)
    all_to_all x1, blocking collectives, local(): lax.all_to_all(current, AXES, split_axis=0, concat_axis=0, tiled=True)  67.5 us
    pallas_call x1, Pallas kernels, local(): pl.pallas_call(lambda *refs: butterfly(*refs, levels=levels), out_shape=j...  15.4 us
    concatenate x1, other arithmetic, local(): current = jnp.concatenate([weights, picks], axis=1)  2.46 us

profile of v3, /device:TPU:1, one launch (start us, length us, event | category | flops | bytes accessed | tf_op | source)
XLA Modules:
  0.0 86.2 jit_solution(1393872214744061997)
XLA Ops:
  0.0 0.7 convert_element_type.24
  0.7 0.1 copy.6
  0.8 2.5 %fusion.1 = bf16[128,136,128]{2,1,0:T(8,128)(2,1)S(1)} fusion(bf16[128,1,8]{2,1,0:T(2,128)(2,1)S(1)} %copy.6, bf16[128,128,128]{2,1,0:T(8,128)(2,1)} %param.4), kind=kLoop, calls=%fused_computation.2 | loop fusion | flops 13369344 | bytes 8652800 | tf_op jit(solution)/shard_map/concatenate | solution.py:75
  3.3 0.0 copy-start
  3.3 0.0 copy-start.1
  3.3 67.5 %all_to_all.5.refs_3_ = bf16[128,136,128]{2,1,0:T(8,128)(2,1)S(1)} all-to-all(bf16[128,136,128]{2,1,0:T(8,128)(2,1)S(1)} %fusion.1), channel_id=1, replica_groups=mesh['wide'=8,'sub'=16] {'wide','sub'}, dimensions={0} | all-to-all | bytes 8912896 | tf_op jit(solution)/shard_map/all_to_all | solution.py:76
  70.8 0.1 slice_convert_fusion
  70.8 0.0 copy-done
  70.8 0.0 copy-done.1
  70.9 15.4 %shard_map.46 = bf16[128,128,128]{2,1,0:T(8,128)(2,1)} custom-call(s32[128,8]{1,0:T(8,128)S(1)} %bitcast.7, s32[8,128]{1,0:T(8,128)S(1)} %bitcast.8, bf16[8,16,128,128]{3,2,1,0:T(8,128)(2,1)S(1)} %copy-done, bf16[128,136,128]{2,1,0:T(8,128)(2,1)S(1)} %all_to_all.5.refs_3_), custom_call_target="tpu_custom_call" | custom-call | flops 8589934592 | bytes 12582912 | tf_op jit(solution)/shard_map/pallas_call | solution.py:81
Async XLA Ops:
  3.3 67.6 %copy-start = (bf16[8,16,128,128]{3,2,1,0:T(8,128)(2,1)S(1)}, bf16[8,16,128,128]{3,2,1,0:T(8,128)(2,1)}, u32[]{:S(2)}) copy-start(bf16[8,16,128,128]{3,2,1,0:T(8,128)(2,1)} %refs_2_.1) | copy-start | bytes 12582916
  3.3 67.5 %copy-start.1 = (s32[4,128,2]{1,2,0:T(2,128)S(1)}, s32[4,128,2]{1,2,0:T(2,128)}, u32[]{:S(2)}) copy-start(s32[4,128,2]{1,2,0:T(2,128)} %param.7) | copy-start | bytes 12292

commit v4 on v3

--- a/solution.py
+++ b/solution.py
@@ -7,13 +7,40 @@
 
 AXES = ("wide", "sub")
 EXTRA = 8
+PARTS = 8
 
 
-def butterfly(first, second, tables, data, out, here, there, out_done, *, levels):
+def pack(place, picks, weights, packed, held, held_done, done):
+    boxes, count, cols = weights.shape
+    copies = []
+    for part in range(PARTS):
+        where = pl.ds(part * (boxes // PARTS), boxes // PARTS)
+        copies.append(pltpu.make_async_copy(weights.at[where], packed.at[where, pl.ds(0, count)], done.at[part]))
+    first = pltpu.make_async_copy(picks, held, held_done)
+    first.start()
+    for copy in copies:
+        copy.start()
+    first.wait()
+    shape = (boxes * EXTRA, boxes)
+    chosen = lax.broadcasted_iota(jnp.int32, shape, 1) == lax.broadcasted_iota(jnp.int32, shape, 0) // EXTRA
+    rows = jnp.where(chosen, jnp.tile(held[...].astype(jnp.float32), (boxes, 1)), 0.0).astype(jnp.bfloat16)
+    column = (lax.broadcasted_iota(jnp.int32, (boxes, cols), 1) == place[0]).astype(jnp.bfloat16)
+    spread = jnp.dot(rows, column, preferred_element_type=jnp.float32)
+    packed[:, count:] = spread.astype(jnp.bfloat16).reshape(boxes, EXTRA, cols)
+    for copy in copies:
+        copy.wait()
+
+
+def butterfly(second, tables, data, out, here, there, picks, first, first_done, out_done, *, levels):
     boxes, count, cols = out.shape
     span = 2**levels
     apart = boxes // span
     half = boxes // 2
+
+    picks[...] = jnp.sum(data[:, count:].astype(jnp.float32), axis=0).astype(jnp.int32)
+    copy = pltpu.make_async_copy(picks, first, first_done)
+    copy.start()
+    copy.wait()
 
     def out_copy(part, row):
         where = pl.ds(row * apart + part * (apart // 2), apart // 2)
@@ -41,7 +68,7 @@
         for level in range(levels):
             flip = 2**level
             lows = [part * half + split(pair, flip) for pair in range(half // 2)]
-            combine(level, [(low, low + flip) for low in lows], lambda term, box: first[box, 2 * level + term])
+            combine(level, [(low, low + flip) for low in lows], lambda term, box: first[2 * level + term, box])
         return 0
 
     def after(part, _):
@@ -51,13 +78,16 @@
                 split(pair // (apart // 2), flip) * apart + part * (apart // 2) + pair % (apart // 2)
                 for pair in range(half // 2)
             ]
-            combine(
-                levels + step,
-                [(low, low + flip * apart) for low in lows],
-                lambda term, box: second[2 * step + term, box],
-            )
-        for row in range(span):
-            out_copy(part, row).start()
+            pieces = 2 if step == levels - 1 else 1
+            for piece in range(pieces):
+                combine(
+                    levels + step,
+                    [(low, low + flip * apart) for low in lows[piece * len(lows) // pieces :][: len(lows) // pieces]],
+                    lambda term, box: second[2 * step + term, box],
+                )
+                if step == levels - 1:
+                    for row in range(piece * span // pieces, (piece + 1) * span // pieces):
+                        out_copy(part, row).start()
         return 0
 
     lax.fori_loop(0, 2, before, 0)
@@ -70,29 +100,44 @@
 def local(weights, tables, pattern_first, pattern_second):
     levels = pattern_first.shape[0]
     boxes, count, cols = weights.shape
-    picks = pattern_first.transpose(1, 0, 2).reshape(boxes, 1, 2 * levels).astype(jnp.bfloat16)
-    picks = jnp.pad(picks, ((0, 0), (0, EXTRA - 1), (0, cols - 2 * levels)))
-    current = jnp.concatenate([weights, picks], axis=1)
-    current = lax.all_to_all(current, AXES, split_axis=0, concat_axis=0, tiled=True)
-    first = current[:, count, : 2 * levels].astype(jnp.int32)
-    second = pattern_second.transpose(0, 2, 1).reshape(2 * levels, boxes)
+    place = lax.axis_index(AXES).astype(jnp.int32).reshape(1)
+    first, second = (
+        pattern.transpose(0, 2, 1).reshape(2 * levels, boxes) for pattern in (pattern_first, pattern_second)
+    )
     smem = pl.BlockSpec(memory_space=pltpu.SMEM)
     vmem = pl.BlockSpec(memory_space=pltpu.VMEM)
+    whole = pl.BlockSpec(memory_space=pl.ANY)
+    current = pl.pallas_call(
+        pack,
+        out_shape=jax.ShapeDtypeStruct((boxes, count + EXTRA, cols), weights.dtype),
+        in_specs=[smem, whole, whole],
+        out_specs=vmem,
+        scratch_shapes=[
+            pltpu.VMEM(first.shape, first.dtype),
+            pltpu.SemaphoreType.DMA,
+            pltpu.SemaphoreType.DMA((PARTS,)),
+        ],
+        compiler_params=pltpu.CompilerParams(vmem_limit_bytes=16 * 2**20),
+    )(place, *(pltpu.with_memory_space_constraint(array, pltpu.HBM) for array in (first, weights)))
+    current = lax.all_to_all(current, AXES, split_axis=0, concat_axis=0, tiled=True)
     return pl.pallas_call(
         lambda *refs: butterfly(*refs, levels=levels),
         out_shape=jax.ShapeDtypeStruct(weights.shape, weights.dtype),
-        in_specs=[smem, smem, vmem, vmem],
-        out_specs=pl.BlockSpec(memory_space=pl.ANY),
+        in_specs=[smem, vmem, vmem],
+        out_specs=whole,
         scratch_shapes=[
             pltpu.VMEM(weights.shape, weights.dtype),
             pltpu.VMEM(weights.shape, weights.dtype),
+            pltpu.VMEM(first.shape, first.dtype),
+            pltpu.SMEM(first.shape, first.dtype),
+            pltpu.SemaphoreType.DMA,
             pltpu.SemaphoreType.DMA((2,)),
         ],
         compiler_params=pltpu.CompilerParams(vmem_limit_bytes=40 * 2**20),
         cost_estimate=pl.CostEstimate(
             flops=2 * levels * boxes * 2 * 2 * 128**3, bytes_accessed=12 * 2**20, transcendentals=0
         ),
-    )(first, second, tables, current)
+    )(second, tables, current)
 
 
 def solution(mesh):

time: 86.4 us -> 84.8 us (0.981)
  other arithmetic: 3.2 us -> 0 us
  Pallas kernels: 15.4 us -> 17.2 us
    concatenate x1 -> x0, other arithmetic: 2.46 us -> none  [local(): current = jnp.concatenate([weights, picks], axis=1)]
    pallas_call x0 -> x1, Pallas kernels: none -> 2.24 us  [local(): pl.pallas_call(pack, out_shape=jax.ShapeDtypeStruct((boxes, count + EXTRA...]
where the time goes in v4:
time: 84.8 us; the launch traced here: 84.7 us
  blocking collectives  67.5 us (80%)
  Pallas kernels  17.2 us (20%)
    all_to_all x1, blocking collectives, local(): lax.all_to_all(current, AXES, split_axis=0, concat_axis=0, tiled=True)  67.5 us
    pallas_call x1, Pallas kernels, local(): pl.pallas_call(lambda *refs: butterfly(*refs, levels=levels), out_shape=j...  14.9 us
    pallas_call x1, Pallas kernels, local(): pl.pallas_call(pack, out_shape=jax.ShapeDtypeStruct((boxes, count + EXTRA...  2.24 us

profile of v4, /device:TPU:1, one launch (start us, length us, event | category | flops | bytes accessed | tf_op | source)
XLA Modules:
  0.0 84.7 jit_solution(1359433618925914663)
XLA Ops:
  0.0 2.2 %shard_map.46 = bf16[128,136,128]{2,1,0:T(8,128)(2,1)S(1)} custom-call(s32[1]{0:T(128)} %bitcast.2.place, s32[8,128]{1,0:T(8,128)} %bitcast.8, bf16[128,128,128]{2,1,0:T(8,128)(2,1)} %weights.1), custom_call_target="tpu_custom_call" | custom-call | tf_op jit(solution)/shard_map/pallas_call | solution.py:110
  2.2 0.0 copy-start
  2.3 0.0 copy-start.1
  2.3 67.5 %all_to_all.5.refs_2_ = bf16[128,136,128]{2,1,0:T(8,128)(2,1)S(1)} all-to-all(bf16[128,136,128]{2,1,0:T(8,128)(2,1)S(1)} %shard_map.46), channel_id=1, replica_groups=mesh['wide'=8,'sub'=16] {'wide','sub'}, dimensions={0} | all-to-all | bytes 8912896 | tf_op jit(solution)/shard_map/all_to_all | solution.py:122
  69.7 0.0 copy-done
  69.7 0.0 copy-done.1
  69.7 14.9 %shard_map.47 = bf16[128,128,128]{2,1,0:T(8,128)(2,1)} custom-call(s32[8,128]{1,0:T(8,128)S(1)} %bitcast.7, bf16[8,16,128,128]{3,2,1,0:T(8,128)(2,1)S(1)} %copy-done, bf16[128,136,128]{2,1,0:T(8,128)(2,1)S(1)} %all_to_all.5.refs_2_), custom_call_target="tpu_custom_call" | custom-call | flops 8589934592 | bytes 12582912 | tf_op jit(solution)/shard_map/pallas_call | solution.py:123
Async XLA Ops:
  2.2 67.5 %copy-start = (bf16[8,16,128,128]{3,2,1,0:T(8,128)(2,1)S(1)}, bf16[8,16,128,128]{3,2,1,0:T(8,128)(2,1)}, u32[]{:S(2)}) copy-start(bf16[8,16,128,128]{3,2,1,0:T(8,128)(2,1)} %refs_1_.1) | copy-start | bytes 12582916
  2.3 67.5 %copy-start.1 = (s32[4,128,2]{1,2,0:T(2,128)S(1)}, s32[4,128,2]{1,2,0:T(2,128)}, u32[]{:S(2)}) copy-start(s32[4,128,2]{1,2,0:T(2,128)} %param.7) | copy-start | bytes 12292

commit v5 on v4

--- a/solution.py
+++ b/solution.py
@@ -31,12 +31,16 @@
         copy.wait()
 
 
-def butterfly(second, tables, data, out, here, there, picks, first, first_done, out_done, *, levels):
+def butterfly(
+    picks_after, tables, data, out, here, there, picks, first, second, first_done, second_done, out_done, *, levels
+):
     boxes, count, cols = out.shape
     span = 2**levels
     apart = boxes // span
     half = boxes // 2
 
+    later = pltpu.make_async_copy(picks_after, second, second_done)
+    later.start()
     picks[...] = jnp.sum(data[:, count:].astype(jnp.float32), axis=0).astype(jnp.int32)
     copy = pltpu.make_async_copy(picks, first, first_done)
     copy.start()
@@ -78,7 +82,7 @@
                 split(pair // (apart // 2), flip) * apart + part * (apart // 2) + pair % (apart // 2)
                 for pair in range(half // 2)
             ]
-            pieces = 2 if step == levels - 1 else 1
+            pieces = 4 if step == levels - 1 else 1
             for piece in range(pieces):
                 combine(
                     levels + step,
@@ -91,6 +95,7 @@
         return 0
 
     lax.fori_loop(0, 2, before, 0)
+    later.wait()
     lax.fori_loop(0, 2, after, 0)
     for part in range(2):
         for row in range(span):
@@ -123,13 +128,15 @@
     return pl.pallas_call(
         lambda *refs: butterfly(*refs, levels=levels),
         out_shape=jax.ShapeDtypeStruct(weights.shape, weights.dtype),
-        in_specs=[smem, vmem, vmem],
+        in_specs=[whole, vmem, vmem],
         out_specs=whole,
         scratch_shapes=[
             pltpu.VMEM(weights.shape, weights.dtype),
             pltpu.VMEM(weights.shape, weights.dtype),
             pltpu.VMEM(first.shape, first.dtype),
             pltpu.SMEM(first.shape, first.dtype),
+            pltpu.SMEM(second.shape, second.dtype),
+            pltpu.SemaphoreType.DMA,
             pltpu.SemaphoreType.DMA,
             pltpu.SemaphoreType.DMA((2,)),
         ],

time: 84.8 us -> 84 us (level)
  no operation moved by 1% of the time
where the time goes in v5:
time: 84 us; the launch traced here: 83.9 us
  blocking collectives  67.5 us (80%)
  Pallas kernels  16.4 us (20%)
    all_to_all x1, blocking collectives, local(): lax.all_to_all(current, AXES, split_axis=0, concat_axis=0, tiled=True)  67.5 us
    pallas_call x1, Pallas kernels, local(): pl.pallas_call(lambda *refs: butterfly(*refs, levels=levels), out_shape=j...  14.2 us
    pallas_call x1, Pallas kernels, local(): pl.pallas_call(pack, out_shape=jax.ShapeDtypeStruct((boxes, count + EXTRA...  2.24 us

profile of v5, /device:TPU:1, one launch (start us, length us, event | category | flops | bytes accessed | tf_op | source)
XLA Modules:
  0.0 83.9 jit_solution(14791758323690942412)
XLA Ops:
  0.0 2.2 %shard_map.46 = bf16[128,136,128]{2,1,0:T(8,128)(2,1)S(1)} custom-call(s32[1]{0:T(128)} %bitcast.2.place, s32[8,128]{1,0:T(8,128)} %bitcast.8, bf16[128,128,128]{2,1,0:T(8,128)(2,1)} %weights.1), custom_call_target="tpu_custom_call" | custom-call | tf_op jit(solution)/shard_map/pallas_call | solution.py:115
  2.2 0.0 copy-start
  2.3 0.0 copy-start.1
  2.3 67.5 %all_to_all.5.refs_2_ = bf16[128,136,128]{2,1,0:T(8,128)(2,1)S(1)} all-to-all(bf16[128,136,128]{2,1,0:T(8,128)(2,1)S(1)} %shard_map.46), channel_id=1, replica_groups=mesh['wide'=8,'sub'=16] {'wide','sub'}, dimensions={0} | all-to-all | bytes 8912896 | tf_op jit(solution)/shard_map/all_to_all | solution.py:127
  69.7 0.0 copy-done
  69.7 0.0 copy-done.1
  69.7 14.2 %shard_map.47 = bf16[128,128,128]{2,1,0:T(8,128)(2,1)} custom-call(s32[8,128]{1,0:T(8,128)S(1)} %bitcast.7, bf16[8,16,128,128]{3,2,1,0:T(8,128)(2,1)S(1)} %copy-done, bf16[128,136,128]{2,1,0:T(8,128)(2,1)S(1)} %all_to_all.5.refs_2_), custom_call_target="tpu_custom_call" | custom-call | flops 8589934592 | bytes 12582912 | tf_op jit(solution)/shard_map/pallas_call | solution.py:128
Async XLA Ops:
  2.2 67.5 %copy-start = (bf16[8,16,128,128]{3,2,1,0:T(8,128)(2,1)S(1)}, bf16[8,16,128,128]{3,2,1,0:T(8,128)(2,1)}, u32[]{:S(2)}) copy-start(bf16[8,16,128,128]{3,2,1,0:T(8,128)(2,1)} %refs_1_.1) | copy-start | bytes 12582916
  2.3 67.5 %copy-start.1 = (s32[4,128,2]{1,2,0:T(2,128)S(1)}, s32[4,128,2]{1,2,0:T(2,128)}, u32[]{:S(2)}) copy-start(s32[4,128,2]{1,2,0:T(2,128)} %param.7) | copy-start | bytes 12292

commit v6 on v5

--- a/solution.py
+++ b/solution.py
@@ -6,33 +6,40 @@
 from jax.sharding import PartitionSpec as P
 
 AXES = ("wide", "sub")
-EXTRA = 8
+EXTRA = 2
 PARTS = 8
 
 
 def pack(place, picks, weights, packed, held, held_done, done):
-    boxes, count, cols = weights.shape
+    boxes, pairs, _, cols = weights.shape
+    groups = held.shape[0] // EXTRA
     copies = []
     for part in range(PARTS):
         where = pl.ds(part * (boxes // PARTS), boxes // PARTS)
-        copies.append(pltpu.make_async_copy(weights.at[where], packed.at[where, pl.ds(0, count)], done.at[part]))
+        copies.append(pltpu.make_async_copy(weights.at[where], packed.at[where, pl.ds(0, pairs)], done.at[part]))
     first = pltpu.make_async_copy(picks, held, held_done)
     first.start()
     for copy in copies:
         copy.start()
     first.wait()
-    shape = (boxes * EXTRA, boxes)
-    chosen = lax.broadcasted_iota(jnp.int32, shape, 1) == lax.broadcasted_iota(jnp.int32, shape, 0) // EXTRA
-    rows = jnp.where(chosen, jnp.tile(held[...].astype(jnp.float32), (boxes, 1)), 0.0).astype(jnp.bfloat16)
-    column = (lax.broadcasted_iota(jnp.int32, (boxes, cols), 1) == place[0]).astype(jnp.bfloat16)
-    spread = jnp.dot(rows, column, preferred_element_type=jnp.float32)
-    packed[:, count:] = spread.astype(jnp.bfloat16).reshape(boxes, EXTRA, cols)
+    row = lax.broadcasted_iota(jnp.int32, (boxes * EXTRA, boxes), 0)
+    chosen = lax.broadcasted_iota(jnp.int32, row.shape, 1) == (row >> 1)
+    column = lax.broadcasted_iota(jnp.int32, (boxes, cols), 1)
+    width = cols // groups
+    values = held[...].astype(jnp.float32)
+    spread = jnp.zeros((boxes * EXTRA, cols), jnp.float32)
+    for group in range(groups):
+        even, odd = values[2 * group : 2 * group + 1], values[2 * group + 1 : 2 * group + 2]
+        rows = jnp.where(chosen, jnp.where((row & 1) == 0, even, odd), 0.0).astype(jnp.bfloat16)
+        target = (column == group * width + (place[0] & (width - 1))).astype(jnp.bfloat16)
+        spread = spread + jnp.dot(rows, target, preferred_element_type=jnp.float32)
+    packed[:, pairs] = spread.astype(jnp.bfloat16).reshape(boxes, EXTRA, cols)
     for copy in copies:
         copy.wait()
 
 
 def butterfly(
-    picks_after, tables, data, out, here, there, picks, first, second, first_done, second_done, out_done, *, levels
+    picks_after, tables, data, message, out, here, there, picks, first, second, first_done, second_done, out_done, *, levels
 ):
     boxes, count, cols = out.shape
     span = 2**levels
@@ -41,7 +48,13 @@
 
     later = pltpu.make_async_copy(picks_after, second, second_done)
     later.start()
-    picks[...] = jnp.sum(data[:, count:].astype(jnp.float32), axis=0).astype(jnp.int32)
+    groups = picks.shape[0] // EXTRA
+    width = boxes // groups
+    sums = [
+        jnp.sum(message[group * width : (group + 1) * width, count // 2].astype(jnp.float32), axis=0)
+        for group in range(groups)
+    ]
+    picks[...] = jnp.concatenate(sums, axis=0).astype(jnp.int32)
     copy = pltpu.make_async_copy(picks, first, first_done)
     copy.start()
     copy.wait()
@@ -50,11 +63,11 @@
         where = pl.ds(row * apart + part * (apart // 2), apart // 2)
         return pltpu.make_async_copy(here.at[where], out.at[where], out_done.at[part])
 
-    def combine(level, pairs, pick):
-        source, target = (there, here) if level % 2 else (here if level else data, there)
+    def combine(level, pairs, pick, read=None):
+        source, target = (there, here) if level % 2 else (here, there)
         done = []
-        for low, high in pairs:
-            rows = jnp.concatenate([source[low, :count], source[high, :count]], axis=1)
+        for index, (low, high) in enumerate(pairs):
+            rows = jnp.concatenate(read(index) if read else [source[low], source[high]], axis=1)
             own = [tables[level, pick(0, box)] for box in (low, high)]
             far = [tables[level, pick(1, box)] for box in (low, high)]
             square = jnp.concatenate(
@@ -72,7 +85,18 @@
         for level in range(levels):
             flip = 2**level
             lows = [part * half + split(pair, flip) for pair in range(half // 2)]
-            combine(level, [(low, low + flip) for low in lows], lambda term, box: first[2 * level + term, box])
+            arrived = data.at[pl.ds(pl.multiple_of(part * half * (count + EXTRA), 128), half * (count + EXTRA))]
+            combine(
+                level,
+                [(low, low + flip) for low in lows],
+                lambda term, box: first[2 * (box // width) + term, level * width + box % width],
+                None
+                if level
+                else lambda index: [
+                    arrived[pl.ds((split(index, flip) + side) * (count + EXTRA), count), :]
+                    for side in (0, flip)
+                ],
+            )
         return 0
 
     def after(part, _):
@@ -114,7 +138,7 @@
     whole = pl.BlockSpec(memory_space=pl.ANY)
     current = pl.pallas_call(
         pack,
-        out_shape=jax.ShapeDtypeStruct((boxes, count + EXTRA, cols), weights.dtype),
+        out_shape=jax.ShapeDtypeStruct((boxes, (count + EXTRA) // 2, 2, cols), weights.dtype),
         in_specs=[smem, whole, whole],
         out_specs=vmem,
         scratch_shapes=[
@@ -123,12 +147,12 @@
             pltpu.SemaphoreType.DMA((PARTS,)),
         ],
         compiler_params=pltpu.CompilerParams(vmem_limit_bytes=16 * 2**20),
-    )(place, *(pltpu.with_memory_space_constraint(array, pltpu.HBM) for array in (first, weights)))
+    )(place, *(pltpu.with_memory_space_constraint(array, pltpu.HBM) for array in (first, weights.reshape(boxes, count // 2, 2, cols))))
     current = lax.all_to_all(current, AXES, split_axis=0, concat_axis=0, tiled=True)
     return pl.pallas_call(
         lambda *refs: butterfly(*refs, levels=levels),
         out_shape=jax.ShapeDtypeStruct(weights.shape, weights.dtype),
-        in_specs=[whole, vmem, vmem],
+        in_specs=[whole, vmem, vmem, vmem],
         out_specs=whole,
         scratch_shapes=[
             pltpu.VMEM(weights.shape, weights.dtype),
@@ -144,7 +168,7 @@
         cost_estimate=pl.CostEstimate(
             flops=2 * levels * boxes * 2 * 2 * 128**3, bytes_accessed=12 * 2**20, transcendentals=0
         ),
-    )(second, tables, current)
+    )(second, tables, current.reshape(boxes * (count + EXTRA), cols), current)
 
 
 def solution(mesh):

time: 84 us -> 82.3 us (0.980)
  blocking collectives: 67.5 us -> 65.6 us
    all_to_all x1, blocking collectives: 67.5 us -> 65.6 us  [local(): lax.all_to_all(current, AXES, split_axis=0, concat_axis=0, tiled=True)]
where the time goes in v6:
time: 82.3 us; the launch traced here: 82.1 us
  blocking collectives  65.6 us (80%)
  Pallas kernels  16.5 us (20%)
    all_to_all x1, blocking collectives, local(): lax.all_to_all(current, AXES, split_axis=0, concat_axis=0, tiled=True)  65.6 us
    pallas_call x1, Pallas kernels, local(): pl.pallas_call(lambda *refs: butterfly(*refs, levels=levels), out_shape=j...  14.2 us
    pallas_call x1, Pallas kernels, local(): pl.pallas_call(pack, out_shape=jax.ShapeDtypeStruct((boxes, (count + EXTR...  2.24 us

profile of v6, /device:TPU:1, one launch (start us, length us, event | category | flops | bytes accessed | tf_op | source)
XLA Modules:
  0.0 82.1 jit_solution(16648209728792585560)
XLA Ops:
  0.0 2.2 %shard_map.46 = bf16[128,65,2,128]{3,2,1,0:T(2,128)(2,1)S(1)} custom-call(s32[1]{0:T(128)} %bitcast.2.place, s32[8,128]{1,0:T(8,128)} %bitcast.12, bf16[128,64,2,128]{3,2,1,0:T(2,128)(2,1)} %bitcast.11), custom_call_target="tpu_custom_call" | custom-call | tf_op jit(solution)/shard_map/pallas_call | solution.py:139
  2.2 0.0 copy-start
  2.3 0.0 copy-start.1
  2.3 65.6 %all_to_all.5.refs_3_ = bf16[128,65,2,128]{3,2,1,0:T(2,128)(2,1)S(1)} all-to-all(bf16[128,65,2,128]{3,2,1,0:T(2,128)(2,1)S(1)} %shard_map.46), channel_id=1, replica_groups=mesh['wide'=8,'sub'=16] {'wide','sub'}, dimensions={0} | all-to-all | bytes 8519680 | tf_op jit(solution)/shard_map/all_to_all | solution.py:151
  67.9 0.0 copy-done
  67.9 0.0 copy-done.1
  67.9 14.2 %shard_map.47 = bf16[128,128,128]{2,1,0:T(8,128)(2,1)} custom-call(s32[8,128]{1,0:T(8,128)S(1)} %bitcast.10, bf16[8,16,128,128]{3,2,1,0:T(8,128)(2,1)S(1)} %copy-done, bf16[16640,128]{1,0:T(8,128)(2,1)S(1)} %bitcast.9, bf16[128,65,2,128]{3,2,1,0:T(2,128)(2,1)S(1)} %all_to_all.5.refs_3_), custom_call_target="tpu_custom_call" | custom-call | flops 8589934592 | bytes 12582912 | tf_op jit(solution)/shard_map/pallas_call | solution.py:152
Async XLA Ops:
  2.2 65.7 %copy-start = (bf16[8,16,128,128]{3,2,1,0:T(8,128)(2,1)S(1)}, bf16[8,16,128,128]{3,2,1,0:T(8,128)(2,1)}, u32[]{:S(2)}) copy-start(bf16[8,16,128,128]{3,2,1,0:T(8,128)(2,1)} %refs_1_.1) | copy-start | bytes 12582916
  2.3 65.7 %copy-start.1 = (s32[4,128,2]{1,2,0:T(2,128)S(1)}, s32[4,128,2]{1,2,0:T(2,128)}, u32[]{:S(2)}) copy-start(s32[4,128,2]{1,2,0:T(2,128)} %param.7) | copy-start | bytes 12292
